TPU v7x, 32 devices: a whole 2x2x4 slice. The times are simulated.
32 devices in a mesh: doc: 8 (over z, y), head: 4 (over x, core).
Axes of the slice: x: 2, y: 2, z: 4, core: 2. Of those that a mesh axis runs over, the one named last changes fastest.
Arguments:
- target_q: bfloat16 [1024, 2048], P('doc', 'head'), may hold values from -300 to 300
- target_kv: bfloat16 [1024, 512], P('doc', 'head'), may hold values from -8 to 8
- doc_kv: bfloat16 [8, 384, 512], P('doc', None, 'head'), may hold values from -6 to 6
- doc_lengths: int32 [8], replicated, may hold values from 1 to 384, 2304 in all
- segment_ids: int32 [1024], replicated, may hold values from 0 to 15, never falling along the last dimension, each value on 1 to 128 neighbouring positions
- out_weight: bfloat16 [2048, 8192], P('head', 'doc'), may hold values from -0.125 to 0.125
Outputs:
- projected: bfloat16 [1024, 8192], P('head', 'doc')
Inputs may be any that keep to these rules, and one draw needn't show every extreme that they name: `segment_ids`: segment numbers never fall along the target rows, and each segment spans at most 128 rows.
All inputs are finite; a program needn't handle non-finite values.
Results may differ from a plain program's by a relative error of at most 0.005.
Values may be sent and summed in bfloat16 or wider, within the bound.
A program may use at most 64 MiB of HBM per device.

v0:
```python
import math
import jax
import jax.numpy as jnp
from jax import lax
from jax.sharding import PartitionSpec as P

masked_score = -1e30


def swapped(array, axis, stride):
    return lax.ppermute(array, axis, [(i, i ^ 1 << stride) for i in range(lax.axis_size(axis))])


def passed_along(value, axis, steps):
    count = lax.axis_size(axis)
    initial, last = (max(0, -steps), min(count, count - steps))
    return lax.ppermute(value, axis, [(source, source + steps) for source in range(initial, last)])


def block_stats(queries, key_block, value_block, visible):
    scaling = 1.0 / math.sqrt(key_block.shape[1])
    scores = (
        lax.dot_general(
            queries, key_block, (((1,), (1,)), ((), ())), preferred_element_type=jnp.float32
        )
        * scaling
    )
    scores = jnp.where(visible, scores, masked_score)
    highest = jnp.max(scores, axis=1)
    weights = jnp.exp(scores - highest[:, None])
    summed = jnp.sum(weights, axis=1)
    blended = jnp.dot(weights.astype(jnp.bfloat16), value_block, preferred_element_type=jnp.float32)
    return (highest, summed, blended)


def merge_stats(state_now, incoming):
    highest = jnp.maximum(state_now[0], incoming[0])
    old_factor = jnp.exp(state_now[0] - highest)
    new_factor = jnp.exp(incoming[0] - highest)
    summed = state_now[1] * old_factor + incoming[1] * new_factor
    blended = state_now[2] * old_factor[:, None] + incoming[2] * new_factor[:, None]
    return (highest, summed, blended)


def body(target_q, target_kv, doc_kv, doc_lengths, segment_ids, out_weight):
    row_count = target_q.shape[0]
    head_dim = target_kv.shape[1]
    per_device = target_q.shape[1] // head_dim
    queries = target_q.reshape(row_count * per_device, head_dim)
    parity = lax.axis_index("head") % 2
    doc_index = lax.axis_index("doc")

    def arrange(own_part, partner):
        return (
            jnp.where(parity == 0, own_part, partner),
            jnp.where(parity == 0, partner, own_part),
        )

    initial = (
        jnp.full((queries.shape[0],), masked_score, jnp.float32),
        jnp.zeros((queries.shape[0],), jnp.float32),
        jnp.zeros((queries.shape[0], head_dim), jnp.float32),
    )
    partner_doc, partner_tgt = swapped((doc_kv, target_kv), "head", 0)
    doc_keys, doc_values = arrange(doc_kv, partner_doc)
    key_docs = lax.all_gather(doc_keys, "doc", axis=0, tiled=True)
    value_docs = lax.all_gather(doc_values, "doc", axis=0, tiled=True)
    slot_index = jnp.arange(key_docs.shape[1], dtype=jnp.int32)

    def attend_doc(doc_step, running):
        key_block = lax.dynamic_index_in_dim(key_docs, doc_step, 0, keepdims=False)
        value_block = lax.dynamic_index_in_dim(value_docs, doc_step, 0, keepdims=False)
        length = lax.dynamic_index_in_dim(doc_lengths, doc_step, 0, keepdims=False)
        visible = (slot_index < length)[None, :]
        return merge_stats(running, block_stats(queries, key_block, value_block, visible))

    stats = lax.fori_loop(0, key_docs.shape[0], attend_doc, initial)
    own_keys, own_values = arrange(target_kv, partner_tgt)
    prev_keys, prev_values = passed_along((own_keys, own_values), "doc", 1)
    own_seg = lax.dynamic_slice_in_dim(segment_ids, doc_index * row_count, row_count)
    prev_start = jnp.maximum(doc_index - 1, 0) * row_count
    prev_seg = jnp.where(
        doc_index > 0, lax.dynamic_slice_in_dim(segment_ids, prev_start, row_count), -1
    )
    token_pos = jnp.arange(row_count, dtype=jnp.int32)
    own_mask = (own_seg[:, None] == own_seg[None, :]) & (token_pos[None, :] <= token_pos[:, None])
    prev_mask = own_seg[:, None] == prev_seg[None, :]
    stats = merge_stats(
        stats, block_stats(queries, own_keys, own_values, jnp.repeat(own_mask, per_device, axis=0))
    )
    stats = merge_stats(
        stats,
        block_stats(queries, prev_keys, prev_values, jnp.repeat(prev_mask, per_device, axis=0)),
    )
    attention = (
        (stats[2] / stats[1][:, None])
        .astype(jnp.bfloat16)
        .reshape(row_count, per_device * head_dim)
    )
    gathered = lax.all_gather(attention, "doc", axis=0, tiled=True)
    result = lax.psum_scatter(
        jnp.dot(gathered, out_weight, preferred_element_type=jnp.float32),
        "head",
        scatter_dimension=0,
        tiled=True,
    )
    return result.astype(jnp.bfloat16)


def solution(mesh):
    placed = (
        P("doc", "head"),
        P("doc", "head"),
        P("doc", None, "head"),
        P(),
        P(),
        P("head", "doc"),
    )
    return jax.shard_map(
        body, mesh=mesh, in_specs=placed, out_specs=P("head", "doc"), check_vma=False
    )
```

profile of v0, /device:TPU:0, one launch (start us, length us, event | category | flops | bytes accessed | tf_op | source)
XLA Modules:
  0.0 207.3 jit_solution(15352952914273228183)
XLA Ops:
  6.5 0.5 collective-permute-start.1
  7.1 0.8 fusion.38
  8.5 1.0 reshape.30
  9.5 1.4 broadcast_select_fusion.3
  10.9 4.9 %collective-permute-start.2 = (bf16[128,128]{1,0:T(8,128)(2,1)S(1)}, bf16[128,128]{1,0:T(8,128)(2,1)S(1)}, u32[]{:S(2)}, u32[]{:S(2)}) collective-permute-start(bf16[128,128]{1,0:T(8,128)(2,1)S(1)} %get-tuple-element.222), channel_id=1, source_target_pairs={{0,4},{4,8},{8,12},{12,16},{16,20},{20,24},{24,28},{1,5},{5,9},{9,... | collective-permute-start | bytes 98312 | tf_op jit(solution)/shard_map/ppermute | solution.py:17
  15.7 4.0 %collective-permute-start.3 = (bf16[128,128]{1,0:T(8,128)(2,1)}, bf16[128,128]{1,0:T(8,128)(2,1)}, u32[]{:S(2)}, u32[]{:S(2)}) collective-permute-start(bf16[128,128]{1,0:T(8,128)(2,1)} %get-tuple-element.223), channel_id=1, source_target_pairs={{0,4},{4,8},{8,12},{12,16},{16,20},{20,24},{24,28},{1,5},{5,9},{9,... | collective-permute-start | bytes 98312 | tf_op jit(solution)/shard_map/ppermute | solution.py:17
  20.0 0.6 fusion.24
  20.8 0.6 fusion.26
  21.5 0.9 broadcast_select_fusion
  22.4 32.1 %all_gather.10 = bf16[8,384,128]{2,1,0:T(8,128)(2,1)S(1)} all-gather(bf16[1,384,128]{2,1,0:T(8,128)(2,1)S(1)} %get-tuple-element.220), channel_id=1, replica_groups=mesh['doc'=8,'head'=4] {'doc'}, dimensions={0}, use_global_device_ids=true | all-gather | bytes 884736 | tf_op jit(solution)/shard_map/all_gather | solution.py:67
  54.5 32.1 %all_gather.9 = bf16[8,384,128]{2,1,0:T(8,128)(2,1)S(1)} all-gather(bf16[1,384,128]{2,1,0:T(8,128)(2,1)S(1)} %get-tuple-element.221), channel_id=1, replica_groups=mesh['doc'=8,'head'=4] {'doc'}, dimensions={0}, use_global_device_ids=true | all-gather | bytes 884736 | tf_op jit(solution)/shard_map/all_gather | solution.py:66
  86.7 21.7 %while.18 = (s32[]{:T(128)}, f32[512]{0:T(512)S(1)}, f32[512]{0:T(512)S(1)}, f32[512,128]{1,0:T(8,128)S(1)}, s32[8]{0:T(128)}, /*index=5*/bf16[8,384,128]{2,1,0:...) while((s32[]{:T(128)}, f32[512]{0:T(512)S(1)}, ...), condition=%wide.region_3.4_spmd.clone, body=%wide.region_0.3_spmd.clone.sunk | while | flops 102305152 | bytes 3240976 | solution.py:77
  86.7 1.2 dynamic_slice.51
  87.9 0.6 iota_compare_fusion.3
  88.9 0.4 fusion.64
  89.4 1.2 dynamic_slice.51
  90.6 0.6 iota_compare_fusion.3
  91.2 0.3 fusion.61
  91.6 0.4 fusion.64
  92.1 1.2 dynamic_slice.51
  93.3 0.6 iota_compare_fusion.3
  93.9 0.3 fusion.61
  94.3 0.4 fusion.64
  94.8 1.2 dynamic_slice.51
  96.0 0.6 iota_compare_fusion.3
  97.1 0.4 fusion.64
  97.5 1.2 dynamic_slice.51
  98.7 0.6 iota_compare_fusion.3
  99.3 0.3 fusion.61
  99.8 0.4 fusion.64
  100.2 1.2 dynamic_slice.51
  101.4 0.6 iota_compare_fusion.3
  102.0 0.3 fusion.61
  102.5 0.4 fusion.64
  102.9 1.2 dynamic_slice.51
  104.2 0.6 iota_compare_fusion.3
  105.2 0.4 fusion.64
  105.6 1.2 dynamic_slice.51
  106.9 0.6 iota_compare_fusion.3
  107.9 0.4 fusion.64
  108.3 0.7 multiply_add_fusion
  109.0 1.0 convolution_multiply_fusion.2
  110.0 1.2 fusion.23
  111.2 0.7 reshape.33
  112.0 38.6 %all-gather.2.cloned.1.call-done = bf16[1024,512]{1,0:T(8,128)(2,1)} async-done(((bf16[128,512]{1,0:T(8,128)(2,1)}), bf16[1024,512]{1,0:T(8,128)(2,1)}) %all-gather.2.cloned.1.call-update) | async-done | bytes 1048592 | tf_op jit(solution)/shard_map/all_gather | solution.py:100
  150.6 4.4 %fusion.41 = f32[1024,1024]{1,0:T(8,128)} fusion(bf16[1024,512]{1,0:T(8,128)(2,1)} %all-gather.2.cloned.1.call-done, bf16[512,1024]{1,0:T(8,128)(2,1)S(1)} %copy-done), kind=kOutput, calls=%fused_computation.62 | convolution fusion | flops 1073741824 | bytes 6291456 | tf_op jit(solution)/shard_map/dot_general | solution.py:102
  155.0 43.4 %reduce-scatter.2.cloned.1.call-done = f32[256,1024]{1,0:T(8,128)} async-done(((f32[1024,1024]{1,0:T(8,128)}), f32[256,1024]{1,0:T(8,128)}) %reduce-scatter.2.cloned.1.call-update) | async-done | bytes 1048592 | tf_op jit(solution)/shard_map/reduce_scatter | solution.py:101
  198.4 2.1 %convert_element_type.20 = bf16[256,1024]{1,0:T(8,128)(2,1)} convert(f32[256,1024]{1,0:T(8,128)} %reduce-scatter.2.cloned.1.call-done) | non-fusion elementwise | flops 262144 | bytes 1572864 | tf_op jit(solution)/shard_map/convert_element_type | solution.py:107
  (41 shorter events, 3.6 us)
Async XLA Ops:
  6.5 144.0 %copy-start = (bf16[512,1024]{1,0:T(8,128)(2,1)S(1)}, bf16[512,1024]{1,0:T(8,128)(2,1)}, u32[]{:S(2)}) copy-start(bf16[512,1024]{1,0:T(8,128)(2,1)} %param.13) | copy-start | bytes 3145732
  6.5 144.0 %all-gather.2.cloned.1.call-start = ((), (), s32[]{:S(2)}) async-start(), calls=%async_computation.1 | async-start | bytes 1179648 | tf_op jit(solution)/shard_map/all_gather | solution.py:100
  6.5 2.9 %collective-permute-start.1 = (bf16[128,128]{1,0:T(8,128)(2,1)}, bf16[128,128]{1,0:T(8,128)(2,1)S(1)}, u32[]{:S(2)}, u32[]{:S(2)}) collective-permute-start(bf16[128,128]{1,0:T(8,128)(2,1)} %param.9), channel_id=1, source_target_pairs={{0,1},{1,0},{2,3},{3,2},{4,5},{5,4},{6,7},{7,6},{8,9},{9,8},{10,11... | collective-permute-start | bytes 98312 | tf_op jit(solution)/shard_map/ppermute | solution.py:11
  7.0 14.5 %collective-permute-start = (bf16[1,384,128]{2,1,0:T(8,128)(2,1)}, bf16[1,384,128]{2,1,0:T(8,128)(2,1)S(1)}, u32[]{:S(2)}, u32[]{:S(2)}) collective-permute-start(bf16[1,384,128]{2,1,0:T(8,128)(2,1)} %param.10), channel_id=1, source_target_pairs={{0,1},{1,0},{2,3},{3,2},{4,5},{5,4},{6,7},{7,6},{8,9},{9,8},{10,11... | collective-permute-start | bytes 294920 | tf_op jit(solution)/shard_map/ppermute | solution.py:11
  10.9 9.8 %collective-permute-start.2 = (bf16[128,128]{1,0:T(8,128)(2,1)S(1)}, bf16[128,128]{1,0:T(8,128)(2,1)S(1)}, u32[]{:S(2)}, u32[]{:S(2)}) collective-permute-start(bf16[128,128]{1,0:T(8,128)(2,1)S(1)} %get-tuple-element.222), channel_id=1, source_target_pairs={{0,4},{4,8},{8,12},{12,16},{16,20},{20,24},{24,28},{1,5},{5,9},{9,... | collective-permute-start | bytes 98312 | tf_op jit(solution)/shard_map/ppermute | solution.py:17
  15.7 93.3 %collective-permute-start.3 = (bf16[128,128]{1,0:T(8,128)(2,1)}, bf16[128,128]{1,0:T(8,128)(2,1)}, u32[]{:S(2)}, u32[]{:S(2)}) collective-permute-start(bf16[128,128]{1,0:T(8,128)(2,1)} %get-tuple-element.223), channel_id=1, source_target_pairs={{0,4},{4,8},{8,12},{12,16},{16,20},{20,24},{24,28},{1,5},{5,9},{9,... | collective-permute-start | bytes 98312 | tf_op jit(solution)/shard_map/ppermute | solution.py:17
  111.9 86.5 %reduce-scatter.2.cloned.1.call-start = ((), (), s32[]{:S(2)}) async-start(), calls=%async_computation.2 | async-start | bytes 5242880 | tf_op jit(solution)/shard_map/reduce_scatter | solution.py:101
Sparse Core Ops, SparseCore 0:
  112.1 38.4 all-gather.1
  155.1 43.2 reduce-scatter.1
where the time goes:
time: 208 us; the launch traced here: 207 us
  waiting for transfers between devices  82 us (39%)
  blocking collectives  64.3 us (31%)
  between operations  13.6 us (7%)
  other arithmetic  13.1 us (6%)
  matrix products  12.6 us (6%)
  local copies, waits for them, and re-layouts  12 us (6%)
  starting transfers between devices  9.46 us (5%)
    reduce_scatter x1, waiting for transfers between devices, body(): lax.psum_scatter(jnp.dot(gathered, out_weight, preferred_element_type=jnp...  43.4 us
    all_gather x1, waiting for transfers between devices, body(): gathered = lax.all_gather(attention, 'doc', axis=0, tiled=True)  38.6 us
    all_gather x1, blocking collectives, body(): key_docs = lax.all_gather(doc_keys, 'doc', axis=0, tiled=True)  32.1 us
    all_gather x1, blocking collectives, body(): value_docs = lax.all_gather(doc_values, 'doc', axis=0, tiled=True)  32.1 us
    dynamic_slice x8, local copies, waits for them, and re-layouts, attend_doc(): length = lax.dynamic_index_in_dim(doc_lengths, doc_step, 0, keepdims=False)  9.87 us
    ppermute x2, starting transfers between devices, passed_along(): lax.ppermute(value, axis, [(source, source + steps) for source in range(i...  8.91 us
    dot_general x10, matrix products, block_stats(): jnp.dot(weights.astype(jnp.bfloat16), value_block, preferred_element_type...  5.52 us
    lt x8, other arithmetic, attend_doc(): visible = (slot_index < length)[None, :]  4.5 us
  transfers between devices with their start and end apart: 6, of which 2 were waited for; matrix products, arithmetic and copies ran while one was open for 14% of the time, Pallas kernels for 0%

commit v1 on v0

--- a/solution.py
+++ b/solution.py
@@ -63,8 +63,11 @@
     )
     partner_doc, partner_tgt = swapped((doc_kv, target_kv), "head", 0)
     doc_keys, doc_values = arrange(doc_kv, partner_doc)
-    key_docs = lax.all_gather(doc_keys, "doc", axis=0, tiled=True)
-    value_docs = lax.all_gather(doc_values, "doc", axis=0, tiled=True)
+    key_docs, value_docs = jnp.split(
+        lax.all_gather(jnp.concatenate([doc_keys, doc_values], axis=1), "doc", axis=0, tiled=True),
+        [doc_keys.shape[1]],
+        axis=1,
+    )
     slot_index = jnp.arange(key_docs.shape[1], dtype=jnp.int32)
 
     def attend_doc(doc_step, running):

time: 208 us -> 181 us (0.87)
  blocking collectives: 64.3 us -> 0 us
  waiting for transfers between devices: 82 us -> 116 us
    all_gather x2 -> x0, blocking collectives: 64.3 us -> none  [the longest x1 32.1 us: body(): key_docs = lax.all_gather(doc_keys, 'doc', axis=0, tiled=True)]
    all_gather x0 -> x1, waiting for transfers between devices: none -> 32.4 us  [body(): lax.all_gather(jnp.concatenate([doc_keys, doc_values], axis=1), 'doc', ax...]
  transfers between devices with their start and end apart: 6 -> 7, of which waited for: 2 -> 4; matrix products, arithmetic and copies ran while one was open for 14% -> 17% of each run, Pallas kernels for 0% -> 0%
where the time goes in v1:
time: 181 us; the launch traced here: 180 us
  waiting for transfers between devices  116 us (64%)
  other arithmetic  14.6 us (8%)
  local copies, waits for them, and re-layouts  13.6 us (8%)
  between operations  13.2 us (7%)
  matrix products  12.6 us (7%)
  starting transfers between devices  9.57 us (5%)
    reduce_scatter x1, waiting for transfers between devices, body(): lax.psum_scatter(jnp.dot(gathered, out_weight, preferred_element_type=jnp...  43.4 us
    all_gather x1, waiting for transfers between devices, body(): gathered = lax.all_gather(attention, 'doc', axis=0, tiled=True)  39.1 us
    all_gather x1, waiting for transfers between devices, body(): lax.all_gather(jnp.concatenate([doc_keys, doc_values], axis=1), 'doc', ax...  32.4 us
    dynamic_slice x8, local copies, waits for them, and re-layouts, attend_doc(): length = lax.dynamic_index_in_dim(doc_lengths, doc_step, 0, keepdims=False)  9.94 us
    ppermute x2, starting transfers between devices, passed_along(): lax.ppermute(value, axis, [(source, source + steps) for source in range(i...  8.61 us
    dot_general x10, matrix products, block_stats(): jnp.dot(weights.astype(jnp.bfloat16), value_block, preferred_element_type...  5.52 us
    lt x8, other arithmetic, attend_doc(): visible = (slot_index < length)[None, :]  5.19 us
    dot_general x1, matrix products, body(): jnp.dot(gathered, out_weight, preferred_element_type=jnp.float32)  4.41 us
  transfers between devices with their start and end apart: 7, of which 4 were waited for; matrix products, arithmetic and copies ran while one was open for 17% of the time, Pallas kernels for 0%

profile of v1, /device:TPU:0, one launch (start us, length us, event | category | flops | bytes accessed | tf_op | source)
XLA Modules:
  0.0 180.0 jit_solution(3824269680605662698)
XLA Ops:
  6.5 0.5 collective-permute-start
  7.0 1.2 collective-permute-done
  8.1 0.9 broadcast_select_fusion.1
  9.1 0.7 pad_maximum_fusion
  9.8 0.4 collective-permute-start.1
  10.2 0.8 fusion.39
  11.7 1.0 reshape.30
  12.7 1.4 broadcast_select_fusion.3
  14.0 4.6 %collective-permute-start.2 = (bf16[128,128]{1,0:T(8,128)(2,1)S(1)}, bf16[128,128]{1,0:T(8,128)(2,1)S(1)}, u32[]{:S(2)}, u32[]{:S(2)}) collective-permute-start(bf16[128,128]{1,0:T(8,128)(2,1)S(1)} %get-tuple-element.224), channel_id=1, source_target_pairs={{0,4},{4,8},{8,12},{12,16},{16,20},{20,24},{24,28},{1,5},{5,9},{9,... | collective-permute-start | bytes 98312 | tf_op jit(solution)/shard_map/ppermute | solution.py:17
  18.6 4.0 %collective-permute-start.3 = (bf16[128,128]{1,0:T(8,128)(2,1)}, bf16[128,128]{1,0:T(8,128)(2,1)}, u32[]{:S(2)}, u32[]{:S(2)}) collective-permute-start(bf16[128,128]{1,0:T(8,128)(2,1)} %get-tuple-element.225), channel_id=1, source_target_pairs={{0,4},{4,8},{8,12},{12,16},{16,20},{20,24},{24,28},{1,5},{5,9},{9,... | collective-permute-start | bytes 98312 | tf_op jit(solution)/shard_map/ppermute | solution.py:17
  22.9 0.7 fusion.24
  23.7 0.6 fusion.26
  24.4 32.4 %all-gather.3.cloned.1.call-done = bf16[8,768,128]{2,1,0:T(8,128)(2,1)} async-done(((bf16[1,768,128]{2,1,0:T(8,128)(2,1)}), bf16[8,768,128]{2,1,0:T(8,128)(2,1)}) %all-gather.3.cloned.1.call-update) | async-done | bytes 1572880 | tf_op jit(solution)/shard_map/all_gather | solution.py:67
  56.8 1.5 fusion.38
  58.3 22.4 %while.18 = (s32[]{:T(128)}, f32[512]{0:T(512)S(1)}, f32[512]{0:T(512)S(1)}, f32[512,128]{1,0:T(8,128)S(1)}, s32[8]{0:T(128)}, /*index=5*/bf16[8,384,128]{2,1,0:...) while((s32[]{:T(128)}, f32[512]{0:T(512)S(1)}, ...), condition=%wide.region_3.4_spmd.clone, body=%wide.region_0.3_spmd.clone.sunk | while | flops 102305152 | bytes 3240976 | solution.py:80
  58.3 1.2 dynamic_slice.51
  59.6 0.6 iota_compare_fusion.3
  60.7 0.4 fusion.65
  61.1 1.2 dynamic_slice.51
  62.4 0.6 iota_compare_fusion.3
  63.5 0.4 fusion.65
  63.9 1.2 dynamic_slice.51
  65.2 0.6 iota_compare_fusion.3
  66.3 0.4 fusion.65
  66.8 1.2 dynamic_slice.51
  68.0 0.6 iota_compare_fusion.3
  68.7 0.3 fusion.62
  69.1 0.4 fusion.65
  69.6 1.2 dynamic_slice.51
  70.8 0.6 iota_compare_fusion.3
  71.9 0.4 fusion.65
  72.4 1.2 dynamic_slice.51
  73.6 0.6 iota_compare_fusion.3
  74.7 0.4 fusion.65
  75.2 1.2 dynamic_slice.51
  76.4 0.6 iota_compare_fusion.3
  77.5 0.4 fusion.65
  78.0 1.2 dynamic_slice.51
  79.2 0.6 iota_compare_fusion.3
  80.3 0.4 fusion.65
  80.8 0.7 multiply_add_fusion
  81.5 1.0 convolution_multiply_fusion.2
  82.5 1.2 fusion.23
  83.6 0.7 reshape.33
  84.5 39.1 %all-gather.5.cloned.1.call-done = bf16[1024,512]{1,0:T(8,128)(2,1)} async-done(((bf16[128,512]{1,0:T(8,128)(2,1)}), bf16[1024,512]{1,0:T(8,128)(2,1)}) %all-gather.5.cloned.1.call-update) | async-done | bytes 1048592 | tf_op jit(solution)/shard_map/all_gather | solution.py:103
  123.5 4.4 %fusion.42 = f32[1024,1024]{1,0:T(8,128)} fusion(bf16[1024,512]{1,0:T(8,128)(2,1)} %all-gather.5.cloned.1.call-done, bf16[512,1024]{1,0:T(8,128)(2,1)S(1)} %copy-done), kind=kOutput, calls=%fused_computation.64 | convolution fusion | flops 1073741824 | bytes 6291456 | tf_op jit(solution)/shard_map/dot_general | solution.py:105
  128.0 43.4 %reduce-scatter.2.cloned.1.call-done = f32[256,1024]{1,0:T(8,128)} async-done(((f32[1024,1024]{1,0:T(8,128)}), f32[256,1024]{1,0:T(8,128)}) %reduce-scatter.2.cloned.1.call-update) | async-done | bytes 1048592 | tf_op jit(solution)/shard_map/reduce_scatter | solution.py:104
  171.4 2.1 %convert_element_type.20 = bf16[256,1024]{1,0:T(8,128)(2,1)} convert(f32[256,1024]{1,0:T(8,128)} %reduce-scatter.2.cloned.1.call-done) | non-fusion elementwise | flops 262144 | bytes 1572864 | tf_op jit(solution)/shard_map/convert_element_type | solution.py:110
  (44 shorter events, 4.4 us)
Async XLA Ops:
  6.5 117.0 %copy-start = (bf16[512,1024]{1,0:T(8,128)(2,1)S(1)}, bf16[512,1024]{1,0:T(8,128)(2,1)}, u32[]{:S(2)}) copy-start(bf16[512,1024]{1,0:T(8,128)(2,1)} %param.13) | copy-start | bytes 3145732
  6.5 50.3 %all-gather.3.cloned.1.call-start = ((), (), s32[]{:S(2)}) async-start(), calls=%async_computation.1 | async-start | bytes 1769472 | tf_op jit(solution)/shard_map/all_gather | solution.py:67
  6.5 1.6 collective-permute-start
  9.8 113.7 %all-gather.5.cloned.1.call-start = ((), (), s32[]{:S(2)}) async-start(), calls=%async_computation.2 | async-start | bytes 1179648 | tf_op jit(solution)/shard_map/all_gather | solution.py:103
  9.8 2.8 %collective-permute-start.1 = (bf16[128,128]{1,0:T(8,128)(2,1)}, bf16[128,128]{1,0:T(8,128)(2,1)S(1)}, u32[]{:S(2)}, u32[]{:S(2)}) collective-permute-start(bf16[128,128]{1,0:T(8,128)(2,1)} %param.9), channel_id=1, source_target_pairs={{0,1},{1,0},{2,3},{3,2},{4,5},{5,4},{6,7},{7,6},{8,9},{9,8},{10,11... | collective-permute-start | bytes 98312 | tf_op jit(solution)/shard_map/ppermute | solution.py:11
  14.0 9.5 %collective-permute-start.2 = (bf16[128,128]{1,0:T(8,128)(2,1)S(1)}, bf16[128,128]{1,0:T(8,128)(2,1)S(1)}, u32[]{:S(2)}, u32[]{:S(2)}) collective-permute-start(bf16[128,128]{1,0:T(8,128)(2,1)S(1)} %get-tuple-element.224), channel_id=1, source_target_pairs={{0,4},{4,8},{8,12},{12,16},{16,20},{20,24},{24,28},{1,5},{5,9},{9,... | collective-permute-start | bytes 98312 | tf_op jit(solution)/shard_map/ppermute | solution.py:17
  18.6 62.8 %collective-permute-start.3 = (bf16[128,128]{1,0:T(8,128)(2,1)}, bf16[128,128]{1,0:T(8,128)(2,1)}, u32[]{:S(2)}, u32[]{:S(2)}) collective-permute-start(bf16[128,128]{1,0:T(8,128)(2,1)} %get-tuple-element.225), channel_id=1, source_target_pairs={{0,4},{4,8},{8,12},{12,16},{16,20},{20,24},{24,28},{1,5},{5,9},{9,... | collective-permute-start | bytes 98312 | tf_op jit(solution)/shard_map/ppermute | solution.py:17
  84.4 87.0 %reduce-scatter.2.cloned.1.call-start = ((), (), s32[]{:S(2)}) async-start(), calls=%async_computation.3 | async-start | bytes 5242880 | tf_op jit(solution)/shard_map/reduce_scatter | solution.py:104
Sparse Core Ops, SparseCore 0:
  9.9 46.8 all-gather.2
  84.5 38.9 all-gather.4
  128.1 43.2 reduce-scatter.1
